TPU v7x, 32 devices: a whole 2x2x4 slice. The times are simulated.
32 devices in a mesh: slab: 16 (over z, y, x), row: 2 (over core).
Axes of the slice: x: 2, y: 2, z: 4, core: 2. Of those that a mesh axis runs over, the one named last changes fastest.
Arguments:
- diag_block: float32 [16, 2, 512, 512], P('slab', None, 'row'), may hold values from -3 to 8
- lower_block: float32 [16, 2, 512, 512], P('slab', None, 'row'), may hold values from -0.4375 to 0.4375
- upper_block: float32 [16, 2, 512, 512], P('slab', None, 'row'), may hold values from -0.4375 to 0.4375
- twist: int32 [16, 512], P('slab'), may hold values from 0 to 511, each once within a row
- excitation: float32 [16, 2, 512, 128], P('slab', None, 'row'), may hold values from -24 to 24
Outputs:
- solution: float32 [16, 2, 512, 128], P('slab', None, 'row')
Inputs may be any that keep to these rules, and one draw needn't show every extreme that they name: Each row of twist is a permutation of 0 to 511.
All inputs are finite; a program needn't handle non-finite values.
Results may differ from a plain program's by a relative error of at most 0.00014.
Values sent between devices are 32-bit elements; how exact they have to be, the bound alone decides.
No kernel may reach another device: no remote copies, remote signals or barrier semaphores. Data moves between devices by JAX's collectives and lax.ppermute only.
A program may use at most 128 MiB of HBM per device.

v0:
```python
import jax
import jax.numpy as jnp
from jax import lax
from jax.sharding import PartitionSpec as P


def from_behind(x, axis, by):
    peers = lax.axis_size(axis)
    pairs = [(i, i + by) for i in range(peers) if 0 <= i + by < peers]
    return lax.ppermute(x, axis, pairs)


def complex_product(left_mat, right_mat):
    exact = lax.Precision.HIGHEST
    real_part = jnp.dot(
        left_mat[0], right_mat[0], precision=exact, preferred_element_type=jnp.float32
    ) - jnp.dot(left_mat[1], right_mat[1], precision=exact, preferred_element_type=jnp.float32)
    imag_part = jnp.dot(
        left_mat[0], right_mat[1], precision=exact, preferred_element_type=jnp.float32
    ) + jnp.dot(left_mat[1], right_mat[0], precision=exact, preferred_element_type=jnp.float32)
    return jnp.stack([real_part, imag_part])


def gather_square(block_rows):
    return lax.all_gather(block_rows, "row", axis=1, tiled=True)


def gather_couplings(upper_rows, lower_rows, drive_rows):
    return (
        lax.all_gather(upper_rows, "row", axis=1, tiled=True),
        lax.all_gather(lower_rows, "row", axis=1, tiled=True),
        lax.all_gather(drive_rows, "row", axis=1, tiled=True),
    )


def slab_neighbor(value, offset):
    return from_behind(value, "slab", offset)


def gather_solution(vector_rows):
    return lax.all_gather(vector_rows, "row", axis=1, tiled=True)


def newton_state(block_rows, row_start, need_full):
    row_count = block_rows.shape[1]
    block_full = gather_square(block_rows)
    order = block_full.shape[2]
    identity = (
        lax.broadcasted_iota(jnp.int32, (order, order), 0)
        == lax.broadcasted_iota(jnp.int32, (order, order), 1)
    ).astype(jnp.float32)
    iterate_full = jnp.stack([0.4 * identity - 0.04 * block_full[0], -0.04 * block_full[1]])
    iterate_rows = lax.dynamic_slice_in_dim(iterate_full, row_start, row_count, 1)
    update = complex_product(complex_product(iterate_rows, block_full), iterate_full)
    iterate_full = gather_square(2.0 * iterate_rows - update)
    iterate_rows = lax.dynamic_slice_in_dim(iterate_full, row_start, row_count, 1)
    product_rows = complex_product(iterate_rows, block_full)
    inverse_rows = 2.0 * iterate_rows - complex_product(product_rows, iterate_full)
    inverse_full = gather_square(inverse_rows) if need_full else inverse_rows
    return (inverse_rows, inverse_full, block_full, product_rows)


def left_apply(left_rows, inverse_state):
    return complex_product(left_rows, inverse_state[1])


def right_apply(inverse_state, vector_full):
    return complex_product(inverse_state[0], vector_full)


def neighbor_solutions(local_rows, distance):
    lower_side = gather_solution(slab_neighbor(local_rows, distance))
    upper_side = gather_solution(slab_neighbor(local_rows, -distance))
    return (lower_side, upper_side)


def body(diag_block, lower_block, upper_block, twist, excitation):
    slab_count = lax.axis_size("slab")
    slab_index = lax.axis_index("slab")
    row_index = lax.axis_index("row")
    diag_rows = diag_block[0]
    row_count = diag_rows.shape[1]
    order = diag_rows.shape[2]
    row_start = row_index * row_count
    strand_order = twist[0]
    lower_twisted = jnp.take(lower_block[0], strand_order, axis=2) * (slab_index > 0).astype(
        jnp.float32
    )
    upper_twisted = jnp.take(upper_block[0], strand_order, axis=2) * (
        slab_index < slab_count - 1
    ).astype(jnp.float32)
    drive_rows = excitation[0]
    even_slab = slab_index % 2 == 0
    fourth_slab = slab_index % 4 == 0
    first_state = newton_state(diag_rows, row_start, True)
    upper_full, lower_full, drive_full = gather_couplings(upper_twisted, lower_twisted, drive_rows)
    toward_upper = left_apply(slab_neighbor(lower_twisted, -1), first_state)
    toward_lower = left_apply(slab_neighbor(upper_twisted, 1), first_state)
    sent_upper = jnp.concatenate(
        [
            complex_product(toward_upper, upper_full),
            complex_product(toward_upper, lower_full),
            complex_product(toward_upper, drive_full),
        ],
        axis=2,
    )
    sent_lower = jnp.concatenate(
        [
            complex_product(toward_lower, upper_full),
            complex_product(toward_lower, lower_full),
            complex_product(toward_lower, drive_full),
        ],
        axis=2,
    )
    from_lower = slab_neighbor(sent_upper, 1)
    from_upper = slab_neighbor(sent_lower, -1)
    diag_one = jnp.where(
        even_slab,
        diag_rows - from_lower[:, :, :order] - from_upper[:, :, order : 2 * order],
        diag_rows,
    )
    lower_one = jnp.where(even_slab, -from_lower[:, :, order : 2 * order], lower_twisted)
    upper_one = jnp.where(even_slab, -from_upper[:, :, :order], upper_twisted)
    drive_one = jnp.where(
        even_slab,
        drive_rows - from_lower[:, :, 2 * order :] - from_upper[:, :, 2 * order :],
        drive_rows,
    )
    second_state = newton_state(diag_one, row_start, True)
    upper_two, lower_two, drive_two = gather_couplings(upper_one, lower_one, drive_one)
    toward_upper = left_apply(slab_neighbor(lower_one, -2), second_state)
    toward_lower = left_apply(slab_neighbor(upper_one, 2), second_state)
    sent_upper = jnp.concatenate(
        [complex_product(toward_upper, upper_two), complex_product(toward_upper, drive_two)], axis=2
    )
    sent_lower = jnp.concatenate(
        [complex_product(toward_lower, lower_two), complex_product(toward_lower, drive_two)], axis=2
    )
    from_lower = slab_neighbor(sent_upper, 2)
    from_upper = slab_neighbor(sent_lower, -2)
    diag_two = jnp.where(
        fourth_slab, diag_one - from_lower[:, :, :order] - from_upper[:, :, :order], diag_one
    )
    drive_coarse = jnp.where(
        fourth_slab, drive_one - from_lower[:, :, order:] - from_upper[:, :, order:], drive_one
    )
    coarse_state = newton_state(diag_two, row_start, False)
    coarse_solution = right_apply(coarse_state, gather_solution(drive_coarse))
    lower_side, upper_side = neighbor_solutions(coarse_solution, 2)
    middle_residual = (
        drive_two - complex_product(lower_two, lower_side) - complex_product(upper_two, upper_side)
    )
    middle_solution = right_apply(second_state, middle_residual)
    even_solution = jnp.where(fourth_slab, coarse_solution, middle_solution)
    lower_side, upper_side = neighbor_solutions(even_solution, 1)
    odd_residual = (
        drive_full
        - complex_product(lower_full, lower_side)
        - complex_product(upper_full, upper_side)
    )
    odd_solution = right_apply(first_state, odd_residual)
    return jnp.where(even_slab, even_solution, odd_solution)[None]


def solution(mesh):
    return jax.shard_map(
        body,
        mesh=mesh,
        in_specs=(
            P("slab", None, "row", None),
            P("slab", None, "row", None),
            P("slab", None, "row", None),
            P("slab", None),
            P("slab", None, "row", None),
        ),
        out_specs=P("slab", None, "row", None),
        check_vma=False,
    )
```

profile of v0, /device:TPU:13, one launch (start us, length us, event | category | flops | bytes accessed | tf_op | source)
XLA Modules:
  0.0 564.7 jit_solution(13398596303713844719)
XLA Ops:
  7.3 14.0 %all-gather.37.cloned.1.call-done = f32[1,2,512,512]{3,2,1,0:T(8,128)} async-done(((f32[1,2,256,512]{3,2,1,0:T(8,128)}), f32[1,2,512,512]{3,2,1,0:T(8,128)}) %all-gather.37.cloned.1.call-update) | async-done | bytes 2097168 | tf_op jit(solution)/shard_map/all_gather | solution.py:25
  33.6 11.6 %all-gather.15.cloned.1.call-done = f32[2,512,512]{2,1,0:T(8,128)} async-done(((f32[2,256,512]{2,1,0:T(8,128)}), f32[2,512,512]{2,1,0:T(8,128)}) %all-gather.15.cloned.1.call-update) | async-done | bytes 2097168 | tf_op jit(solution)/shard_map/all_gather | solution.py:25
  57.0 3.1 gather_fusion
  62.9 3.3 gather_fusion.1
  70.5 3.2 collective-permute-start
  79.0 40.9 %collective-permute-done = f32[2,256,512]{2,1,0:T(8,128)S(1)} collective-permute-done((f32[2,256,512]{2,1,0:T(8,128)}, f32[2,256,512]{2,1,0:T(8,128)S(1)}, u32[]{:S(2)}, u32[]{:S(2)}) %collective-permute-start) | collective-permute-done | bytes 1048608 | tf_op jit(solution)/shard_map/ppermute | solution.py:10
  140.9 3.4 fusion.123
  170.1 3.5 collective-permute-start.1
  173.6 88.8 %collective-permute-done.3 = f32[2,256,1152]{2,1,0:T(8,128)} collective-permute-done((f32[2,256,1152]{2,1,0:T(8,128)}, f32[2,256,1152]{2,1,0:T(8,128)}, u32[]{:S(2)}, u32[]{:S(2)}) %collective-permute-start.3) | collective-permute-done | bytes 2359328 | tf_op jit(solution)/shard_map/ppermute | solution.py:10
  262.4 4.3 fusion.47
  267.1 12.3 %all-gather.23.cloned.1.call-done = f32[2,512,512]{2,1,0:T(8,128)} async-done(((f32[2,256,512]{2,1,0:T(8,128)}), f32[2,512,512]{2,1,0:T(8,128)}) %all-gather.23.cloned.1.call-update) | async-done | bytes 2097168 | tf_op jit(solution)/shard_map/all_gather | solution.py:25
  293.2 11.4 %all-gather.25.cloned.1.call-done = f32[2,512,512]{2,1,0:T(8,128)} async-done(((f32[2,256,512]{2,1,0:T(8,128)}), f32[2,512,512]{2,1,0:T(8,128)}) %all-gather.25.cloned.1.call-update) | async-done | bytes 2097168 | tf_op jit(solution)/shard_map/all_gather | solution.py:25
  318.5 4.0 collective-permute-start.6
  323.8 3.1 all_gather.67
  326.9 36.4 %collective-permute-done.4 = f32[2,256,512]{2,1,0:T(8,128)S(1)} collective-permute-done((f32[2,256,512]{2,1,0:T(8,128)S(1)}, f32[2,256,512]{2,1,0:T(8,128)S(1)}, u32[]{:S(2)}, u32[]{:S(2)}) %collective-permute-start.4) | collective-permute-done | bytes 1048608 | tf_op jit(solution)/shard_map/ppermute | solution.py:10
  380.8 5.2 collective-permute-start.5
  406.4 35.0 %collective-permute-done.5 = f32[2,256,640]{2,1,0:T(8,128)} collective-permute-done((f32[2,256,640]{2,1,0:T(8,128)}, f32[2,256,640]{2,1,0:T(8,128)}, u32[]{:S(2)}, u32[]{:S(2)}) %collective-permute-start.5) | collective-permute-done | bytes 1310752 | tf_op jit(solution)/shard_map/ppermute | solution.py:10
  446.1 12.8 %all-gather.33.cloned.1.call-done = f32[2,512,512]{2,1,0:T(8,128)} async-done(((f32[2,256,512]{2,1,0:T(8,128)}), f32[2,512,512]{2,1,0:T(8,128)}) %all-gather.33.cloned.1.call-update) | async-done | bytes 2097168 | tf_op jit(solution)/shard_map/all_gather | solution.py:25
  475.7 8.5 %all-gather.35.cloned.1.call-done = f32[2,512,512]{2,1,0:T(8,128)} async-done(((f32[2,256,512]{2,1,0:T(8,128)}), f32[2,512,512]{2,1,0:T(8,128)}) %all-gather.35.cloned.1.call-update) | async-done | bytes 2097168 | tf_op jit(solution)/shard_map/all_gather | solution.py:25
  498.7 4.0 collective-permute-start.8
  502.7 7.1 %collective-permute-done.9 = f32[2,256,128]{2,1,0:T(8,128)S(1)} collective-permute-done((f32[2,256,128]{2,1,0:T(8,128)S(1)}, f32[2,256,128]{2,1,0:T(8,128)S(1)}, u32[]{:S(2)}, u32[]{:S(2)}) %collective-permute-start.9) | collective-permute-done | bytes 262176 | tf_op jit(solution)/shard_map/ppermute | solution.py:10
  525.6 5.0 collective-permute-start.11
  532.5 3.3 collective-permute-done.11
  535.9 8.0 %all_gather.75 = f32[2,512,128]{2,1,0:T(8,128)S(1)} all-gather(f32[2,256,128]{2,1,0:T(8,128)S(1)} %collective-permute-done.11), channel_id=1, replica_groups=mesh['slab'=16,'row'=2] {'row'}, dimensions={1}, use_global_device_ids=true | all-gather | bytes 786432 | tf_op jit(solution)/shard_map/all_gather | solution.py:41
  (301 shorter events, 216.6 us)
Async XLA Ops:
  6.5 14.8 %all-gather.37.cloned.1.call-start = ((), (), s32[]{:S(2)}) async-start(), calls=%async_computation.11 | async-start | bytes 3145728 | tf_op jit(solution)/shard_map/all_gather | solution.py:25
  7.3 38.0 %all-gather.15.cloned.1.call-start = ((), (), s32[]{:S(2)}) async-start(), calls=%async_computation | async-start | bytes 3145728 | tf_op jit(solution)/shard_map/all_gather | solution.py:25
  33.4 86.5 %all-gather.17.cloned.1.call-start = ((), (), s32[]{:S(2)}) async-start(), calls=%async_computation.1 | async-start | bytes 3145728 | tf_op jit(solution)/shard_map/all_gather | solution.py:25
  56.2 84.7 %all-gather.21.cloned.1.call-start = ((), (), s32[]{:S(2)}) async-start(), calls=%async_computation.3 | async-start | bytes 3145728 | tf_op jit(solution)/shard_map/all_gather | solution.py:31
  70.5 76.7 %all-gather.19.cloned.1.call-start = ((), (), s32[]{:S(2)}) async-start(), calls=%async_computation.2 | async-start | bytes 3145728 | tf_op jit(solution)/shard_map/all_gather | solution.py:30
  70.5 49.4 %collective-permute-start = (f32[2,256,512]{2,1,0:T(8,128)}, f32[2,256,512]{2,1,0:T(8,128)S(1)}, u32[]{:S(2)}, u32[]{:S(2)}) collective-permute-start(f32[2,256,512]{2,1,0:T(8,128)} %get-tuple-element.13), channel_id=1, source_target_pairs={{2,0},{4,2},{6,4},{8,6},{10,8},{12,10},{14,12},{16,14},{18,16},{20... | collective-permute-start | bytes 3145736 | tf_op jit(solution)/shard_map/ppermute | solution.py:10
  73.8 54.3 %collective-permute-start.2 = (f32[2,256,512]{2,1,0:T(8,128)S(1)}, f32[2,256,512]{2,1,0:T(8,128)}, u32[]{:S(2)}, u32[]{:S(2)}) collective-permute-start(f32[2,256,512]{2,1,0:T(8,128)S(1)} %get-tuple-element.14), channel_id=1, source_target_pairs={{0,2},{2,4},{4,6},{6,8},{8,10},{10,12},{12,14},{14,16},{16,18},{18... | collective-permute-start | bytes 3145736 | tf_op jit(solution)/shard_map/ppermute | solution.py:10
  76.0 203.4 %all-gather.23.cloned.1.call-start = ((), (), s32[]{:S(2)}) async-start(), calls=%async_computation.4 | async-start | bytes 3145728 | tf_op jit(solution)/shard_map/all_gather | solution.py:25
  157.8 104.6 %collective-permute-start.3 = (f32[2,256,1152]{2,1,0:T(8,128)}, f32[2,256,1152]{2,1,0:T(8,128)}, u32[]{:S(2)}, u32[]{:S(2)}) collective-permute-start(f32[2,256,1152]{2,1,0:T(8,128)} %maximum_maximum_fusion.1), channel_id=1, source_target_pairs={{2,0},{4,2},{6,4},{8,6},{10,8},{12,10},{14,12},{16,14},{18,16},{20... | collective-permute-start | bytes 7077896 | tf_op jit(solution)/shard_map/ppermute | solution.py:10
  170.1 92.3 %collective-permute-start.1 = (f32[2,256,1152]{2,1,0:T(8,128)}, f32[2,256,1152]{2,1,0:T(8,128)}, u32[]{:S(2)}, u32[]{:S(2)}) collective-permute-start(f32[2,256,1152]{2,1,0:T(8,128)} %maximum_maximum_fusion), channel_id=1, source_target_pairs={{0,2},{2,4},{4,6},{6,8},{8,10},{10,12},{12,14},{14,16},{16,18},{18... | collective-permute-start | bytes 7077896 | tf_op jit(solution)/shard_map/ppermute | solution.py:10
  266.8 37.8 %all-gather.25.cloned.1.call-start = ((), (), s32[]{:S(2)}) async-start(), calls=%async_computation.5 | async-start | bytes 3145728 | tf_op jit(solution)/shard_map/all_gather | solution.py:25
  292.7 71.6 %all-gather.27.cloned.1.call-start = ((), (), s32[]{:S(2)}) async-start(), calls=%async_computation.6 | async-start | bytes 3145728 | tf_op jit(solution)/shard_map/all_gather | solution.py:25
  315.6 56.5 %all-gather.29.cloned.1.call-start = ((), (), s32[]{:S(2)}) async-start(), calls=%async_computation.7 | async-start | bytes 3145728 | tf_op jit(solution)/shard_map/all_gather | solution.py:30
  316.3 81.2 %all-gather.31.cloned.1.call-start = ((), (), s32[]{:S(2)}) async-start(), calls=%async_computation.8 | async-start | bytes 3145728 | tf_op jit(solution)/shard_map/all_gather | solution.py:31
  316.4 47.0 %collective-permute-start.4 = (f32[2,256,512]{2,1,0:T(8,128)S(1)}, f32[2,256,512]{2,1,0:T(8,128)S(1)}, u32[]{:S(2)}, u32[]{:S(2)}) collective-permute-start(f32[2,256,512]{2,1,0:T(8,128)S(1)} %copy-done.35), channel_id=1, source_target_pairs={{4,0},{6,2},{8,4},{10,6},{12,8},{14,10},{16,12},{18,14},{20,16},{2... | collective-permute-start | bytes 3145736 | tf_op jit(solution)/shard_map/ppermute | solution.py:10
  318.5 67.5 %collective-permute-start.6 = (f32[2,256,512]{2,1,0:T(8,128)}, f32[2,256,512]{2,1,0:T(8,128)}, u32[]{:S(2)}, u32[]{:S(2)}) collective-permute-start(f32[2,256,512]{2,1,0:T(8,128)} %get-tuple-element.8), channel_id=1, source_target_pairs={{0,4},{2,6},{4,8},{6,10},{8,12},{10,14},{12,16},{14,18},{16,20},{1... | collective-permute-start | bytes 3145736 | tf_op jit(solution)/shard_map/ppermute | solution.py:10
  322.6 136.3 %all-gather.33.cloned.1.call-start = ((), (), s32[]{:S(2)}) async-start(), calls=%async_computation.9 | async-start | bytes 3145728 | tf_op jit(solution)/shard_map/all_gather | solution.py:25
  380.8 60.6 %collective-permute-start.5 = (f32[2,256,640]{2,1,0:T(8,128)}, f32[2,256,640]{2,1,0:T(8,128)}, u32[]{:S(2)}, u32[]{:S(2)}) collective-permute-start(f32[2,256,640]{2,1,0:T(8,128)} %maximum_maximum_fusion.2), channel_id=1, source_target_pairs={{0,4},{2,6},{4,8},{6,10},{8,12},{10,14},{12,16},{14,18},{16,20},{1... | collective-permute-start | bytes 3932168 | tf_op jit(solution)/shard_map/ppermute | solution.py:10
  404.5 38.2 %collective-permute-start.7 = (f32[2,256,640]{2,1,0:T(8,128)}, f32[2,256,640]{2,1,0:T(8,128)}, u32[]{:S(2)}, u32[]{:S(2)}) collective-permute-start(f32[2,256,640]{2,1,0:T(8,128)} %maximum_maximum_fusion.3), channel_id=1, source_target_pairs={{4,0},{6,2},{8,4},{10,6},{12,8},{14,10},{16,12},{18,14},{20,16},{2... | collective-permute-start | bytes 3932168 | tf_op jit(solution)/shard_map/ppermute | solution.py:10
  445.7 38.5 %all-gather.35.cloned.1.call-start = ((), (), s32[]{:S(2)}) async-start(), calls=%async_computation.10 | async-start | bytes 3145728 | tf_op jit(solution)/shard_map/all_gather | solution.py:25
  496.5 13.3 %collective-permute-start.9 = (f32[2,256,128]{2,1,0:T(8,128)S(1)}, f32[2,256,128]{2,1,0:T(8,128)S(1)}, u32[]{:S(2)}, u32[]{:S(2)}) collective-permute-start(f32[2,256,128]{2,1,0:T(8,128)S(1)} %pad_maximum_fusion), channel_id=1, source_target_pairs={{4,0},{6,2},{8,4},{10,6},{12,8},{14,10},{16,12},{18,14},{20,16},{2... | collective-permute-start | bytes 786440 | tf_op jit(solution)/shard_map/ppermute | solution.py:10
  498.7 16.1 %collective-permute-start.8 = (f32[2,256,128]{2,1,0:T(8,128)S(1)}, f32[2,256,128]{2,1,0:T(8,128)S(1)}, u32[]{:S(2)}, u32[]{:S(2)}) collective-permute-start(f32[2,256,128]{2,1,0:T(8,128)S(1)} %pad_maximum_fusion), channel_id=1, source_target_pairs={{0,4},{2,6},{4,8},{6,10},{8,12},{10,14},{12,16},{14,18},{16,20},{1... | collective-permute-start | bytes 786440 | tf_op jit(solution)/shard_map/ppermute | solution.py:10
  525.6 10.3 %collective-permute-start.11 = (f32[2,256,128]{2,1,0:T(8,128)S(1)}, f32[2,256,128]{2,1,0:T(8,128)S(1)}, u32[]{:S(2)}, u32[]{:S(2)}) collective-permute-start(f32[2,256,128]{2,1,0:T(8,128)S(1)} %maximum_select_fusion.1), channel_id=1, source_target_pairs={{2,0},{4,2},{6,4},{8,6},{10,8},{12,10},{14,12},{16,14},{18,16},{20... | collective-permute-start | bytes 786440 | tf_op jit(solution)/shard_map/ppermute | solution.py:10
  530.6 15.3 %collective-permute-start.10 = (f32[2,256,128]{2,1,0:T(8,128)S(1)}, f32[2,256,128]{2,1,0:T(8,128)S(1)}, u32[]{:S(2)}, u32[]{:S(2)}) collective-permute-start(f32[2,256,128]{2,1,0:T(8,128)S(1)} %maximum_select_fusion.1), channel_id=1, source_target_pairs={{0,2},{2,4},{4,6},{6,8},{8,10},{10,12},{12,14},{14,16},{16,18},{18... | collective-permute-start | bytes 786440 | tf_op jit(solution)/shard_map/ppermute | solution.py:10
  (45 other events, 533.6 us)
Sparse Core Ops, SparseCore 0:
  8.9 12.4 all-gather.36
  33.5 11.7 all-gather.14
  56.3 11.7 all-gather.16
  70.6 11.7 all-gather.20
  83.8 11.7 all-gather.18
  266.9 12.4 all-gather.22
  292.8 11.7 all-gather.24
  315.7 12.1 all-gather.26
  329.4 11.3 all-gather.28
  342.2 11.7 all-gather.30
  445.8 13.0 all-gather.32
  472.4 11.7 all-gather.34
where the time goes:
time: 573 us; the launch traced here: 565 us
  waiting for transfers between devices  285 us (50%)
  matrix products  154 us (27%)
  starting transfers between devices  39.2 us (7%)
  other arithmetic  30.4 us (5%)
  blocking collectives  23.9 us (4%)
  local copies, waits for them, and re-layouts  16.5 us (3%)
  between operations  15.7 us (3%)
    ppermute x12, waiting for transfers between devices, from_behind(): return lax.ppermute(x, axis, pairs)  213 us
    all_gather x8, waiting for transfers between devices, gather_square(): return lax.all_gather(block_rows, 'row', axis=1, tiled=True)  70.6 us
    dot_general x33, matrix products, complex_product(): jnp.dot(left_mat[0], right_mat[1], precision=exact, preferred_element_typ...  43.4 us
    dot_general x33, matrix products, complex_product(): jnp.dot(left_mat[0], right_mat[0], precision=exact, preferred_element_typ...  39.1 us
    dot_general x33, matrix products, complex_product(): jnp.dot(left_mat[1], right_mat[1], precision=exact, preferred_element_typ...  38 us
    ppermute x12, starting transfers between devices, from_behind(): return lax.ppermute(x, axis, pairs)  37.4 us
    dot_general x33, matrix products, complex_product(): jnp.dot(left_mat[1], right_mat[0], precision=exact, preferred_element_typ...  33.5 us
    all_gather x5, blocking collectives, gather_solution(): return lax.all_gather(vector_rows, 'row', axis=1, tiled=True)  17.8 us
  transfers between devices with their start and end apart: 24, of which 13 were waited for; matrix products, arithmetic and copies ran while one was open for 16% of the time, Pallas kernels for 0%

commit v1 on v0

v1 whole, which is shorter than its diff:
```python
import functools

import jax
import jax.numpy as jnp
from jax import lax
from jax.experimental import pallas as pl
from jax.experimental.pallas import tpu as pltpu
from jax.sharding import PartitionSpec as P

F32 = jnp.float32
BF16 = jnp.bfloat16
TILE = 256


def halves(x):
    high = x.astype(BF16)
    return high, (x - high.astype(F32)).astype(BF16)


def put(high, low, rows, cols, real, imag):
    for part, value in enumerate((real, imag, real + imag)):
        h, l = halves(value)
        high[part, rows, cols] = h
        low[part, rows, cols] = l


def dot(a, b):
    return jnp.dot(a, b, preferred_element_type=F32)


def product(ah, al, bh, bl, cols, rows=slice(None)):
    terms = []
    for part in range(3):
        xh, xl = ah[part, rows, :], al[part, rows, :]
        yh, yl = bh[part, :, cols], bl[part, :, cols]
        terms.append(dot(xh, yh) + dot(xh, yl) + dot(xl, yh))
    first, second, third = terms
    return first - second, third - first - second


def apply(ah, al, real, imag, rows=slice(None)):
    width = real.shape[1]
    vh, vl = halves(jnp.concatenate([real, imag], axis=1))
    sides = []
    for part in range(2):
        xh, xl = ah[part, rows, :], al[part, rows, :]
        sides.append(dot(xh, vh) + dot(xh, vl) + dot(xl, vh))
    first, second = sides
    return (
        first[:, :width] - second[:, width:],
        first[:, width:] + second[:, :width],
    )


def eye(rows, cols, row_start, col_start):
    return (
        lax.broadcasted_iota(jnp.int32, (rows, cols), 0) + row_start
        == lax.broadcasted_iota(jnp.int32, (rows, cols), 1) + col_start
    ).astype(F32)


def tiles(width, start=0):
    def run(step):
        if width % TILE:
            for begin in range(0, width, 128):
                step(pl.ds(start + begin, 128), begin)
            return

        @pl.loop(0, width // TILE)
        def _(index):
            begin = pl.multiple_of(index * TILE, TILE)
            step(pl.ds(pl.multiple_of(start + begin, 128), TILE), begin)

    return run


def twist_kernel(info, lower, upper, order, drive, diag, first, second, joined, coarse):
    strands = lower.shape[2]
    pick = (
        lax.broadcasted_iota(jnp.int32, (strands, strands), 0) == order[...]
    ).astype(BF16)
    is_a = info[1] == 1
    width = drive.shape[2]
    for part in range(2):
        moved = []
        for source in (lower, upper):
            value = source[part]
            high, rest = halves(value)
            middle, low = halves(value - high.astype(F32))
            moved.append(dot(high, pick) + dot(middle, pick) + dot(low, pick))
        one = jnp.where(is_a, moved[1], moved[0])
        two = jnp.where(is_a, moved[0], moved[1])
        first[part] = one
        second[part] = two
        joined[part, :, :strands] = one
        joined[part, :, strands : strands + width] = drive[part]
        joined[part, :, strands + width :] = two
        coarse[part, :, :strands] = diag[part]
        coarse[part, :, strands:] = drive[part]


def load_step(info, own, other, mf, mh, ml):
    count = own.shape[1]
    strands = mf.shape[2]
    here = pl.multiple_of(info[0] * count, count)
    there = pl.multiple_of((1 - info[0]) * count, count)
    for start, source in ((here, own), (there, other)):
        rows = pl.ds(start, count)
        real = eye(count, strands, start, 0) - 0.2 * source[0, :, :strands]
        imag = -0.2 * source[1, :, :strands]
        mf[0, rows, :] = real
        mf[1, rows, :] = imag
        put(mh, ml, rows, slice(None), real, imag)


def square(mh, ml, nf, nh, nl):
    @tiles(mh.shape[2])
    def _(cols, begin):
        real, imag = product(mh, ml, mh, ml, cols)
        if nf is not None:
            nf[0, :, cols] = real
            nf[1, :, cols] = imag
        put(nh, nl, slice(None), cols, real, imag)


def inverse(mf, mh, ml, nf, nh, nl, qh, ql, fh, fl, finish):
    strands = mh.shape[2]

    @tiles(strands)
    def _(cols, begin):
        real, imag = product(mh, ml, nh, nl, cols)
        real = real + mf[0, :, cols] + nf[0, :, cols] + eye(strands, TILE, 0, begin)
        imag = imag + mf[1, :, cols] + nf[1, :, cols]
        mf[0, :, cols] = real
        mf[1, :, cols] = imag
        put(qh, ql, slice(None), cols, real, imag)

    square(nh, nl, None, fh, fl)

    @tiles(strands)
    def _(cols, begin):
        real, imag = product(fh, fl, qh, ql, cols)
        finish(cols, 0.2 * (real + mf[0, :, cols]), 0.2 * (imag + mf[1, :, cols]))


def first_kernel(
    info, own, other, wide_own, wide_other, reh, rel,
    mf, mh, ml, nf, nh, nl, qh, ql, fh, fl, wh, wl,
):
    load_step(info, own, other, mf, mh, ml)
    count = own.shape[1]
    strands = mh.shape[2]
    here = pl.multiple_of(info[0] * count, count)
    there = pl.multiple_of((1 - info[0]) * count, count)
    for start, source in ((here, wide_own), (there, wide_other)):
        put(wh, wl, pl.ds(start, count), slice(None), source[0], source[1])
    square(mh, ml, nf, nh, nl)

    def finish(cols, real, imag):
        put(mh, ml, slice(None), cols, real, imag)

    inverse(mf, mh, ml, nf, nh, nl, qh, ql, fh, fl, finish)
    width = wh.shape[2] - 2 * strands

    def spread(cols, begin):
        real, imag = product(mh, ml, wh, wl, cols)
        put(reh, rel, slice(None), cols, real, imag)

    tiles(strands)(spread)
    tiles(width, strands)(spread)
    tiles(strands, strands + width)(spread)


def couple_kernel(begin_col, info, one, two, reh, rel, out, ch, cl):
    swap = info[1] == 1
    real = jnp.where(swap, one[0], two[0])
    imag = jnp.where(swap, one[1], two[1])
    put(ch, cl, slice(None), slice(None), real, imag)

    def step(cols, begin):
        real, imag = product(ch, cl, reh, rel, cols)
        place = pl.ds(begin, cols.size)
        out[0, :, place] = real
        out[1, :, place] = imag

    total = out.shape[2]
    whole = total // TILE * TILE
    done = 0
    for width in (whole, total - whole):
        if width:
            def shifted(cols, begin, done=done):
                step(cols, begin + done)

            tiles(width, begin_col + done)(shifted)
            done += width


def step_right(source, gh, gl, bh, bl, target, base):
    put(gh, gl, slice(None), slice(None), source[0], source[1])

    @tiles(target.shape[2])
    def _(cols, begin):
        real, imag = product(gh, gl, bh, bl, cols)
        if base is not None:
            real = real + base[0, :, cols]
            imag = imag + base[1, :, cols]
        target[0, :, cols] = real
        target[1, :, cols] = imag


def second_kernel(
    info, own, other, kc_own, kc_other, far, base, out, mf, mh, ml, nh, nl, kch, kcl,
    g, k, gh, gl, bh, bl,
):
    load_step(info, own, other, mf, mh, ml)
    count = own.shape[1]
    strands = mh.shape[2]
    width = own.shape[2] - strands
    here = pl.multiple_of(info[0] * count, count)
    there = pl.multiple_of((1 - info[0]) * count, count)
    every = slice(None)
    for start, source, side in ((here, kc_own, own), (there, kc_other, other)):
        rows = pl.ds(start, count)
        put(kch, kcl, rows, every, source[0], source[1])
        put(bh, bl, rows, every, side[0, :, strands:], side[1, :, strands:])
    square(mh, ml, None, nh, nl)
    g[...] = far[:, :, :strands]
    step_right(g, gh, gl, mh, ml, k, g)
    step_right(k, gh, gl, nh, nl, g, k)
    step_right(g, gh, gl, nh, nl, k, None)
    step_right(k, gh, gl, nh, nl, k, g)
    put(gh, gl, every, every, 0.2 * k[0], 0.2 * k[1])

    @tiles(strands)
    def _(cols, begin):
        real, imag = product(gh, gl, kch, kcl, cols)
        source = pl.ds(pl.multiple_of(strands + width + begin, 128), TILE)
        out[0, :, cols] = base[0, :, cols] - far[0, :, source] - real
        out[1, :, cols] = base[1, :, cols] - far[1, :, source] - imag

    real, imag = product(gh, gl, bh, bl, every)
    side = pl.ds(strands, width)
    out[0, :, side] = base[0, :, side] - far[0, :, side] + real
    out[1, :, side] = base[1, :, side] - far[1, :, side] + imag


def shadow_kernel(
    info, mf, mh, ml, nh, nl, reh, rel, zh, zl, pf, qh, ql, fh, fl, yh, yl,
):
    count = zh.shape[1] // 2
    strands = mh.shape[2]
    here = pl.ds(pl.multiple_of(info[0] * count, count), count)
    every = slice(None)

    @tiles(strands)
    def _(cols, begin):
        real, imag = product(mh, ml, nh, nl, cols)
        square_real = nh[0, :, cols].astype(F32) + nl[0, :, cols].astype(F32)
        square_imag = nh[1, :, cols].astype(F32) + nl[1, :, cols].astype(F32)
        real = real + mf[0, :, cols] + square_real + eye(strands, TILE, 0, begin)
        imag = imag + mf[1, :, cols] + square_imag
        pf[0, :, cols] = real
        pf[1, :, cols] = imag
        put(qh, ql, every, cols, real, imag)

    square(nh, nl, None, fh, fl)

    @tiles(strands)
    def _(cols, begin):
        real, imag = product(fh, fl, qh, ql, cols)
        put(
            yh, yl, every, cols,
            0.2 * (real + pf[0, :, cols]), 0.2 * (imag + pf[1, :, cols]),
        )

    zh[:, :count, :] = yh[:, here, :]
    zl[:, :count, :] = yl[:, here, :]

    @tiles(strands)
    def _(cols, begin):
        real, imag = product(
            reh.at[:, :, pl.ds(0, strands)], rel.at[:, :, pl.ds(0, strands)],
            yh, yl, cols, here,
        )
        put(zh, zl, pl.ds(count, count), cols, real, imag)


def coarse_kernel(info, own, other, kch, kcl, fine, xh, xl, xr, vr, mf, mh, ml, bf):
    load_step(info, own, other, mf, mh, ml)
    count = own.shape[1]
    strands = mh.shape[2]
    here = pl.multiple_of(info[0] * count, count)
    there = pl.multiple_of((1 - info[0]) * count, count)
    for start, source in ((here, own), (there, other)):
        bf[:, pl.ds(start, count), :] = source[:, :, strands:]
    real, imag = bf[0], bf[1]
    for _ in range(7):
        real, imag = apply(mh, ml, real, imag)
        real = bf[0] + real
        imag = bf[1] + imag
    real = 0.2 * real
    imag = 0.2 * imag
    rows = pl.ds(here, count)
    bf[0] = real
    bf[1] = imag
    xr[...] = bf[:, rows, :]
    high, low = halves(jnp.concatenate([real, imag], axis=1))
    xh[...] = high
    xl[...] = low
    real, imag = apply(kch, kcl, real, imag, rows)
    vr[0] = fine[0, :, strands:] + real
    vr[1] = fine[1, :, strands:] + imag
    vr[2] = real
    vr[3] = imag


def apply_held(ah, al, vh, vl, rows, cols):
    width = vh.shape[1] // 2
    sides = []
    for part in range(2):
        a, b = ah[part, rows, cols], al[part, rows, cols]
        sides.append(dot(a, vh[...]) + dot(a, vl[...]) + dot(b, vh[...]))
    first, second = sides
    return (
        first[:, :width] - second[:, width:],
        first[:, width:] + second[:, :width],
    )


def last_kernel(info, own, other, zh, zl, reh, rel, xh, xl, middle, odd, vf):
    count = own.shape[1]
    strands = zh.shape[2]
    width = own.shape[2]
    here = pl.multiple_of(info[0] * count, count)
    there = pl.multiple_of((1 - info[0]) * count, count)
    for start, source in ((here, own), (there, other)):
        vf[:, pl.ds(start, count), :] = source[...]
    real, imag = apply(zh, zl, vf[0], vf[1])
    middle[0] = real[:count]
    middle[1] = imag[:count]
    rows = pl.ds(here, count)
    side = pl.ds(strands, width)
    tail = pl.ds(strands + width, strands)
    far_real, far_imag = apply_held(reh, rel, xh, xl, rows, tail)
    near = [
        reh[part, rows, side].astype(F32) + rel[part, rows, side].astype(F32)
        for part in range(2)
    ]
    odd[0] = near[0] - far_real - real[count:]
    odd[1] = near[1] - far_imag - imag[count:]


VMEM = pl.BlockSpec(memory_space=pltpu.VMEM)
SMEM = pl.BlockSpec(memory_space=pltpu.SMEM)


def call(kernel, info, arrays, outs, scratch, flops):
    shapes = [jax.ShapeDtypeStruct(shape, dtype) for shape, dtype in outs]
    moved = sum(x.size * x.dtype.itemsize for x in list(arrays) + shapes)
    return pl.pallas_call(
        kernel,
        out_shape=shapes,
        in_specs=[SMEM] + [VMEM] * len(arrays),
        out_specs=[VMEM] * len(outs),
        scratch_shapes=[pltpu.VMEM(shape, dtype) for shape, dtype in scratch],
        compiler_params=pltpu.CompilerParams(vmem_limit_bytes=58 * 2**20),
        cost_estimate=pl.CostEstimate(
            flops=int(flops), bytes_accessed=int(moved), transcendentals=0
        ),
    )(info, *arrays)


def body(diag_block, lower_block, upper_block, twist, excitation):
    slabs = lax.axis_size("slab")
    slab = lax.axis_index("slab")
    row = lax.axis_index("row")
    diag, lower, upper, drive = diag_block[0], lower_block[0], upper_block[0], excitation[0]
    count, strands = diag.shape[1:]
    width = drive.shape[2]
    narrow = strands + width
    wide = strands + narrow
    info = jnp.stack([row, (slab % 4 == 1).astype(row.dtype)]).astype(jnp.int32)
    unit = 18 * strands**3

    def pairs(phase, by):
        return [
            (i, i + by) for i in range(slabs) if i % 4 == phase and 0 <= i + by < slabs
        ]

    def send(x, *moves):
        return lax.ppermute(x, "slab", [pair for move in moves for pair in pairs(*move)])

    def cross(x):
        return lax.ppermute(x, "row", [(0, 1), (1, 0)])

    def after(x, *gates):
        return lax.optimization_barrier((x,) + gates)[0]

    part = (2, count, strands)
    full = (2, strands, strands)
    trio = (3, strands, strands)
    half = (3, count, strands)
    diag_other = cross(diag)
    first, second, joined, coarse = call(
        twist_kernel, info, [lower, upper, twist, drive, diag],
        [(part, F32), (part, F32), ((2, count, wide), F32), ((2, count, narrow), F32)],
        [], unit / 3,
    )
    near_a = send(first, (2, -1))
    near_b = send(second, (2, 1))
    joined_other = cross(joined)
    reh, rel = call(
        first_kernel, info, [diag, diag_other, joined, joined_other],
        [((3, strands, wide), BF16)] * 2,
        [(full, F32), (trio, BF16), (trio, BF16)] * 2
        + [(trio, BF16)] * 4 + [((3, strands, wide), BF16)] * 2,
        unit * 6.25,
    )
    base_near_a = send(coarse, (2, -1))
    base_near_b = send(coarse, (2, 1))
    second_gate = after(second, reh)
    far_a = send(second_gate, (0, 1))
    far_b = send(after(first, reh), (0, -1))
    base_far = send(after(coarse, far_a), (0, 1))
    pieces = [(half, BF16)] * 2
    (sent,) = call(
        functools.partial(couple_kernel, 0), info, [near_a, near_b, reh, rel],
        [((2, count, narrow), F32)], pieces, unit * 0.625,
    )
    got = send(sent, (1, 2), (3, -2))
    (keep,) = call(
        functools.partial(couple_kernel, narrow), info, [near_a, near_b, reh, rel],
        [(part, F32)], pieces, unit * 0.5,
    )
    keep_other = cross(keep)
    (far,) = call(
        functools.partial(couple_kernel, 0), info, [far_a, far_b, reh, rel],
        [((2, count, wide), F32)], pieces, unit * 1.125,
    )
    fine = base_near_a + base_near_b - sent - got
    fine_other = cross(fine)
    out, mf, mh, ml, nh, nl, kch, kcl = call(
        second_kernel, info,
        [fine, fine_other, keep, keep_other, far, base_far],
        [((2, count, narrow), F32), (full, F32)] + [(trio, BF16)] * 6,
        [(part, F32)] * 2 + pieces + [((3, strands, width), BF16)] * 2,
        unit * 3.625,
    )
    out_got = send(out, (3, 2), (1, -2))
    zh, zl = call(
        shadow_kernel, info, [mf, mh, ml, nh, nl, reh, rel],
        [(trio, BF16)] * 2, [(full, F32)] + [(trio, BF16)] * 6, unit * 3.5,
    )
    total = out + out_got
    total_other = cross(total)
    xh, xl, xr, vr = call(
        coarse_kernel, info, [total, total_other, kch, kcl, fine],
        [((strands, 2 * width), BF16)] * 2
        + [((2, count, width), F32), ((4, count, width), F32)],
        [(full, F32), (trio, BF16), (trio, BF16), ((2, strands, width), F32)],
        unit * 2.5,
    )
    v_got = send(vr[2:], (1, 2), (3, -2))
    x_even = send(xr, (1, -1))
    v = vr[:2] + v_got
    v_other = cross(v)
    middle, odd = call(
        last_kernel, info, [v, v_other, zh, zl, reh, rel, xh, xl],
        [((2, count, width), F32)] * 2, [((2, strands, width), F32)], unit * 0.5,
    )
    x_middle = send(middle, (3, -1))
    return jnp.where(slab % 2 == 1, odd, x_even + x_middle)[None]


def solution(mesh):
    return jax.shard_map(
        body,
        mesh=mesh,
        in_specs=(
            P("slab", None, "row", None),
            P("slab", None, "row", None),
            P("slab", None, "row", None),
            P("slab", None),
            P("slab", None, "row", None),
        ),
        out_specs=P("slab", None, "row", None),
        check_vma=False,
    )
```

time: 573 us -> 328 us (0.57)
  matrix products: 154 us -> 0 us
  Pallas kernels: 0 us -> 117 us
  waiting for transfers between devices: 285 us -> 175 us
  other arithmetic: 30.4 us -> 5.53 us
  blocking collectives: 23.9 us -> 0 us
  starting transfers between devices: 39.2 us -> 19.6 us
  between operations: 15.7 us -> 0.74 us
  local copies, waits for them, and re-layouts: 16.5 us -> 6.86 us
    dot_general x132 -> x0, matrix products: 154 us -> none  [the longest x33 43.4 us: complex_product(): jnp.dot(left_mat[0], right_mat[1], precision=exact, preferred_element_typ...]
    pallas_call x0 -> x9, Pallas kernels: none -> 117 us  [call(): pl.pallas_call(kernel, out_shape=shapes, in_specs=[SMEM] + [VMEM] * len(a...]
    all_gather x12 -> x0, waiting for transfers between devices: 70.6 us -> none  [the longest x8 70.6 us: gather_square(): return lax.all_gather(block_rows, 'row', axis=1, tiled=True)]
    ppermute x12 -> x18, waiting for transfers between devices: 213 us -> 175 us  [the longest x12 172 us: send(): lax.ppermute(x, 'slab', [pair for move in moves for pair in pairs(*move)])]
    all_gather x7 -> x0, blocking collectives: 23.9 us -> none  [the longest x5 17.8 us: gather_solution(): return lax.all_gather(vector_rows, 'row', axis=1, tiled=True)]
    ppermute x12 -> x18, starting transfers between devices: 37.4 us -> 19.6 us  [the longest x12 16.5 us: send(): lax.ppermute(x, 'slab', [pair for move in moves for pair in pairs(*move)])]
    select_n x7 -> x0, other arithmetic: 10.3 us -> none  [the longest x1 4.34 us: body(): jnp.where(even_slab, -from_lower[:, :, order:2 * order], lower_twisted)]
    gather x4 -> x0, local copies, waits for them, and re-layouts: 9.62 us -> none  [the longest x2 4.95 us: body(): jnp.take(upper_block[0], strand_order, axis=2)]
  transfers between devices with their start and end apart: 24 -> 18, of which waited for: 13 -> 4; matrix products, arithmetic and copies ran while one was open for 16% -> 1% of each run, Pallas kernels for 0% -> 24%
where the time goes in v1:
time: 328 us; the launch traced here: 325 us
  waiting for transfers between devices  175 us (53%)
  Pallas kernels  117 us (36%)
  starting transfers between devices  19.6 us (6%)
  local copies, waits for them, and re-layouts  6.86 us (2%)
  other arithmetic  5.53 us (2%)
    ppermute x12, waiting for transfers between devices, send(): lax.ppermute(x, 'slab', [pair for move in moves for pair in pairs(*move)])  172 us
    pallas_call x9, Pallas kernels, call(): pl.pallas_call(kernel, out_shape=shapes, in_specs=[SMEM] + [VMEM] * len(a...  117 us
    ppermute x12, starting transfers between devices, send(): lax.ppermute(x, 'slab', [pair for move in moves for pair in pairs(*move)])  16.5 us
  transfers between devices with their start and end apart: 18, of which 4 were waited for; matrix products, arithmetic and copies ran while one was open for 1% of the time, Pallas kernels for 24%

profile of v1, /device:TPU:13, one launch (start us, length us, event | category | flops | bytes accessed | tf_op | source)
XLA Modules:
  0.0 324.9 jit_solution(10488068547283699795)
XLA Ops:
  0.7 6.7 %shard_map.55 = (f32[2,256,512]{2,1,0:T(8,128)}, f32[2,256,512]{2,1,0:T(8,128)}, f32[2,256,1152]{2,1,0:T(8,128)}, f32[2,256,640]{2,1,0:T(8,128)}) custom-call(s32[2]{0:T(128)} %pad_add_fusion.info, f32[2,256,512]{2,1,0:T(8,128)} %bitcast.8, f32[2,256,512]{2,1,0:T(8,128)} %bitcast.9, s32[1,512]{1,0:T(1,128)} %order.1, f32[2,256,128]{2,1,0:T(8,128)} %bitcast.13, ...), custom_call_target="tpu_custom_call" | custom-call | flops 805306368 | bytes 9177088 | tf_op jit(solution)/shard_map/pallas_call | solution.py:360
  8.1 3.2 collective-permute-start.1
  11.2 1.4 collective-permute-start
  12.6 1.4 collective-permute-start.2
  15.0 2.8 collective-permute-start.3
  17.9 28.3 %shard_map.56 = (bf16[3,512,1152]{2,1,0:T(8,128)(2,1)}, bf16[3,512,1152]{2,1,0:T(8,128)(2,1)}) custom-call(s32[2]{0:T(128)} %pad_add_fusion.info, f32[2,256,512]{2,1,0:T(8,128)} %bitcast.11, f32[2,256,512]{2,1,0:T(8,128)} %copy-done.12, f32[2,256,1152]{2,1,0:T(8,128)} %get-tuple-element.33.wide_own, f32[2,256,1152]{2,1,0:T(8,128)} %collective-permute-done.5.wide_other), custom_call_target="tpu_custom_call" | custom-call | flops 15099494400 | bytes 13893632 | tf_op jit(solution)/shard_map/pallas_call | solution.py:360
  46.1 43.6 %collective-permute-done.2.one = f32[2,256,512]{2,1,0:T(8,128)S(1)} collective-permute-done((f32[2,256,512]{2,1,0:T(8,128)}, f32[2,256,512]{2,1,0:T(8,128)S(1)}, u32[]{:S(2)}, u32[]{:S(2)}) %collective-permute-start.2) | collective-permute-done | bytes 1048608 | tf_op jit(solution)/shard_map/ppermute | solution.py:391
  89.7 22.5 %collective-permute-done.3.two = f32[2,256,512]{2,1,0:T(8,128)S(1)} collective-permute-done((f32[2,256,512]{2,1,0:T(8,128)}, f32[2,256,512]{2,1,0:T(8,128)S(1)}, u32[]{:S(2)}, u32[]{:S(2)}) %collective-permute-start.3) | collective-permute-done | bytes 1048608 | tf_op jit(solution)/shard_map/ppermute | solution.py:391
  113.2 7.6 %shard_map.57 = f32[2,256,640]{2,1,0:T(8,128)} custom-call(s32[2]{0:T(128)} %pad_add_fusion.info, f32[2,256,512]{2,1,0:T(8,128)} %copy-done, f32[2,256,512]{2,1,0:T(8,128)} %copy-done.1, bf16[3,512,1152]{2,1,0:T(8,128)(2,1)} %get-tuple-element.34.reh, bf16[3,512,1152]{2,1,0:T(8,128)(2,1)} %get-tuple-element.35.rel), custom_call_target="tpu_custom_call" | custom-call | flops 1509949440 | bytes 10485760 | tf_op jit(solution)/shard_map/pallas_call | solution.py:360
  122.3 2.0 collective-permute-start.11
  124.3 1.7 subtract_subtract_fusion.own.fine
  126.0 1.3 collective-permute-start.7
  128.0 6.6 %shard_map.58.kc_own = f32[2,256,512]{2,1,0:T(8,128)} custom-call(s32[2]{0:T(128)} %pad_add_fusion.info, f32[2,256,512]{2,1,0:T(8,128)} %copy-done, f32[2,256,512]{2,1,0:T(8,128)} %copy-done.1, bf16[3,512,1152]{2,1,0:T(8,128)(2,1)} %get-tuple-element.34.reh, bf16[3,512,1152]{2,1,0:T(8,128)(2,1)} %get-tuple-element.35.rel), custom_call_target="tpu_custom_call" | custom-call | flops 1207959552 | bytes 10223616 | tf_op jit(solution)/shard_map/pallas_call | solution.py:360
  135.6 9.4 %shard_map.59.far = f32[2,256,1152]{2,1,0:T(8,128)} custom-call(s32[2]{0:T(128)} %pad_add_fusion.info, f32[2,256,512]{2,1,0:T(8,128)} %copy-done.5, f32[2,256,512]{2,1,0:T(8,128)} %copy-done.6, bf16[3,512,1152]{2,1,0:T(8,128)(2,1)} %get-tuple-element.34.reh, bf16[3,512,1152]{2,1,0:T(8,128)(2,1)} %get-tuple-element.35.rel), custom_call_target="tpu_custom_call" | custom-call | flops 2717908992 | bytes 11534336 | tf_op jit(solution)/shard_map/pallas_call | solution.py:360
  145.1 1.1 copy-done.10
  146.2 21.5 %shard_map.60 = (f32[2,256,640]{2,1,0:T(8,128)}, f32[2,512,512]{2,1,0:T(8,128)}, bf16[3,512,512]{2,1,0:T(8,128)(2,1)}, bf16[3,512,512]{2,1,0:T(8,128)(2,1)}, bf1...) custom-call(s32[2]{0:T(128)} %pad_add_fusion.info, ...), custom_call_target="tpu_custom_call" | custom-call | flops 8757706752 | bytes 21233664 | tf_op jit(solution)/shard_map/pallas_call | solution.py:360
  168.7 1.5 add.22.own
  170.8 2.7 collective-permute-done.13.other
  173.4 1.1 copy-done.11
  174.5 11.9 %shard_map.61 = (bf16[512,256]{1,0:T(8,128)(2,1)}, bf16[512,256]{1,0:T(8,128)(2,1)}, f32[2,256,128]{2,1,0:T(8,128)}, f32[4,256,128]{2,1,0:T(8,128)}) custom-call(s32[2]{0:T(128)} %pad_add_fusion.info, f32[2,256,640]{2,1,0:T(8,128)} %copy-done.3, f32[2,256,640]{2,1,0:T(8,128)} %copy-done.11, bf16[3,512,512]{2,1,0:T(8,128)(2,1)} %get-tuple-element.40.kch, ...), custom_call_target="tpu_custom_call" | custom-call | flops 6039797760 | bytes 8388608 | tf_op jit(solution)/shard_map/pallas_call | solution.py:360
  189.5 18.8 %shard_map.62 = (bf16[3,512,512]{2,1,0:T(8,128)(2,1)}, bf16[3,512,512]{2,1,0:T(8,128)(2,1)}) custom-call(s32[2]{0:T(128)} %pad_add_fusion.info, f32[2,512,512]{2,1,0:T(8,128)} %get-tuple-element.43.mf, bf16[3,512,512]{2,1,0:T(8,128)(2,1)} %get-tuple-element.44.mh, bf16[3,512,512]{2,1,0:T(8,128)(2,1)} %get-tuple-element.45.ml, ...), custom_call_target="tpu_custom_call" | custom-call | flops 8455716864 | bytes 18612224 | tf_op jit(solution)/shard_map/pallas_call | solution.py:360
  209.7 6.3 %shard_map.63 = (f32[2,256,128]{2,1,0:T(8,128)}, f32[2,256,128]{2,1,0:T(8,128)}) custom-call(s32[2]{0:T(128)} %pad_add_fusion.info, f32[2,256,128]{2,1,0:T(8,128)} %copy-done.7, f32[2,256,128]{2,1,0:T(8,128)} %copy-done.8, bf16[3,512,512]{2,1,0:T(8,128)(2,1)} %get-tuple-element.48.zh, bf16[3,512,512]{2,1,0:T(8,128)(2,1)} %get-tuple-element.49.zl, ...), custom_call_target="tpu_custom_call" | custom-call | flops 1207959552 | bytes 11796480 | tf_op jit(solution)/shard_map/pallas_call | solution.py:360
  216.0 1.3 collective-permute-start.17
  217.3 106.4 %collective-permute-done.17 = f32[2,256,128]{2,1,0:T(8,128)S(1)} collective-permute-done((f32[2,256,128]{2,1,0:T(8,128)}, f32[2,256,128]{2,1,0:T(8,128)S(1)}, u32[]{:S(2)}, u32[]{:S(2)}) %collective-permute-start.17) | collective-permute-done | bytes 262176 | tf_op jit(solution)/shard_map/ppermute | solution.py:391
  (55 shorter events, 13.4 us)
Async XLA Ops:
  0.7 7.3 %copy-start.4 = (f32[1,2,256,512]{3,2,1,0:T(8,128)S(1)}, f32[1,2,256,512]{3,2,1,0:T(8,128)}, u32[]{:S(2)}) copy-start(f32[1,2,256,512]{3,2,1,0:T(8,128)} %param.5) | copy-start | bytes 3145732
  7.3 10.5 %collective-permute-start.5 = (f32[2,256,1152]{2,1,0:T(8,128)}, f32[2,256,1152]{2,1,0:T(8,128)}, u32[]{:S(2)}, u32[]{:S(2)}) collective-permute-start(f32[2,256,1152]{2,1,0:T(8,128)} %get-tuple-element.33.wide_own), channel_id=1, source_target_pairs={{0,1},{1,0},{2,3},{3,2},{4,5},{5,4},{6,7},{7,6},{8,9},{9,8},{10,11... | collective-permute-start | bytes 7077896 | tf_op jit(solution)/shard_map/ppermute | solution.py:394
  8.0 6.0 %collective-permute-start.4 = (f32[2,256,512]{2,1,0:T(8,128)S(1)}, f32[2,256,512]{2,1,0:T(8,128)S(1)}, u32[]{:S(2)}, u32[]{:S(2)}) collective-permute-start(f32[2,256,512]{2,1,0:T(8,128)S(1)} %bitcast.12), channel_id=1, source_target_pairs={{0,1},{1,0},{2,3},{3,2},{4,5},{5,4},{6,7},{7,6},{8,9},{9,8},{10,11... | collective-permute-start | bytes 3145736 | tf_op jit(solution)/shard_map/ppermute | solution.py:394
  8.1 116.2 %collective-permute-start.1 = (f32[2,256,640]{2,1,0:T(8,128)}, f32[2,256,640]{2,1,0:T(8,128)S(1)}, u32[]{:S(2)}, u32[]{:S(2)}) collective-permute-start(f32[2,256,640]{2,1,0:T(8,128)} %get-tuple-element.38), channel_id=1, source_target_pairs={{4,6},{12,14},{20,22},{28,30},{5,7},{13,15},{21,23},{29,31}} | collective-permute-start | bytes 3932168 | tf_op jit(solution)/shard_map/ppermute | solution.py:391
  11.2 113.0 %collective-permute-start = (f32[2,256,640]{2,1,0:T(8,128)}, f32[2,256,640]{2,1,0:T(8,128)S(1)}, u32[]{:S(2)}, u32[]{:S(2)}) collective-permute-start(f32[2,256,640]{2,1,0:T(8,128)} %get-tuple-element.38), channel_id=1, source_target_pairs={{4,2},{12,10},{20,18},{28,26},{5,3},{13,11},{21,19},{29,27}} | collective-permute-start | bytes 3932168 | tf_op jit(solution)/shard_map/ppermute | solution.py:391
  12.6 77.1 %collective-permute-start.2 = (f32[2,256,512]{2,1,0:T(8,128)}, f32[2,256,512]{2,1,0:T(8,128)S(1)}, u32[]{:S(2)}, u32[]{:S(2)}) collective-permute-start(f32[2,256,512]{2,1,0:T(8,128)} %get-tuple-element.37), channel_id=1, source_target_pairs={{4,2},{12,10},{20,18},{28,26},{5,3},{13,11},{21,19},{29,27}} | collective-permute-start | bytes 3145736 | tf_op jit(solution)/shard_map/ppermute | solution.py:391
  15.0 97.2 %collective-permute-start.3 = (f32[2,256,512]{2,1,0:T(8,128)}, f32[2,256,512]{2,1,0:T(8,128)S(1)}, u32[]{:S(2)}, u32[]{:S(2)}) collective-permute-start(f32[2,256,512]{2,1,0:T(8,128)} %get-tuple-element.36), channel_id=1, source_target_pairs={{4,6},{12,14},{20,22},{28,30},{5,7},{13,15},{21,23},{29,31}} | collective-permute-start | bytes 3145736 | tf_op jit(solution)/shard_map/ppermute | solution.py:391
  89.7 22.5 %copy-start = (f32[2,256,512]{2,1,0:T(8,128)}, f32[2,256,512]{2,1,0:T(8,128)S(1)}, u32[]{:S(2)}) copy-start(f32[2,256,512]{2,1,0:T(8,128)S(1)} %collective-permute-done.2.one) | copy-start | bytes 3145732
  113.2 9.1 %copy-start.9 = (f32[2,256,640]{2,1,0:T(8,128)S(1)}, f32[2,256,640]{2,1,0:T(8,128)}, u32[]{:S(2)}) copy-start(f32[2,256,640]{2,1,0:T(8,128)} %get-tuple-element.38) | copy-start | bytes 3932164
  120.8 3.5 %collective-permute-start.6 = (f32[2,256,640]{2,1,0:T(8,128)}, f32[2,256,640]{2,1,0:T(8,128)S(1)}, u32[]{:S(2)}, u32[]{:S(2)}) collective-permute-start(f32[2,256,640]{2,1,0:T(8,128)} %shard_map.57), channel_id=1, source_target_pairs={{2,6},{10,14},{18,22},{26,30},{6,2},{14,10},{22,18},{30,26},{3,7},... | collective-permute-start | bytes 3932168 | tf_op jit(solution)/shard_map/ppermute | solution.py:391
  121.5 0.7 collective-permute-start.9
  122.3 22.8 %collective-permute-start.11 = (f32[2,256,640]{2,1,0:T(8,128)S(1)}, f32[2,256,640]{2,1,0:T(8,128)}, u32[]{:S(2)}, u32[]{:S(2)}) collective-permute-start(f32[2,256,640]{2,1,0:T(8,128)S(1)} %copy-done.9), channel_id=1, source_target_pairs={{0,2},{8,10},{16,18},{24,26},{1,3},{9,11},{17,19},{25,27}} | collective-permute-start | bytes 3932168 | tf_op jit(solution)/shard_map/ppermute | solution.py:391
  126.0 8.7 %copy-start.2 = (f32[2,256,640]{2,1,0:T(8,128)}, f32[2,256,640]{2,1,0:T(8,128)S(1)}, u32[]{:S(2)}) copy-start(f32[2,256,640]{2,1,0:T(8,128)S(1)} %subtract_subtract_fusion.own.fine) | copy-start | bytes 3932164
  126.0 19.1 %collective-permute-start.7 = (f32[2,256,640]{2,1,0:T(8,128)S(1)}, f32[2,256,640]{2,1,0:T(8,128)S(1)}, u32[]{:S(2)}, u32[]{:S(2)}) collective-permute-start(f32[2,256,640]{2,1,0:T(8,128)S(1)} %subtract_subtract_fusion.own.fine), channel_id=1, source_target_pairs={{0,1},{1,0},{2,3},{3,2},{4,5},{5,4},{6,7},{7,6},{8,9},{9,8},{10,11... | collective-permute-start | bytes 3932168 | tf_op jit(solution)/shard_map/ppermute | solution.py:394
  127.3 7.3 %collective-permute-start.10 = (f32[2,256,512]{2,1,0:T(8,128)}, f32[2,256,512]{2,1,0:T(8,128)S(1)}, u32[]{:S(2)}, u32[]{:S(2)}) collective-permute-start(f32[2,256,512]{2,1,0:T(8,128)} %get-tuple-element.37), channel_id=1, source_target_pairs={{8,6},{16,14},{24,22},{9,7},{17,15},{25,23}} | collective-permute-start | bytes 3145736 | tf_op jit(solution)/shard_map/ppermute | solution.py:391
  134.6 10.4 %collective-permute-start.8 = (f32[2,256,512]{2,1,0:T(8,128)}, f32[2,256,512]{2,1,0:T(8,128)}, u32[]{:S(2)}, u32[]{:S(2)}) collective-permute-start(f32[2,256,512]{2,1,0:T(8,128)} %shard_map.58.kc_own), channel_id=1, source_target_pairs={{0,1},{1,0},{2,3},{3,2},{4,5},{5,4},{6,7},{7,6},{8,9},{9,8},{10,11... | collective-permute-start | bytes 3145736 | tf_op jit(solution)/shard_map/ppermute | solution.py:394
  167.7 1.0 collective-permute-start.12
  170.2 3.2 collective-permute-start.13
  187.4 0.7 collective-permute-start.14
  189.1 19.2 %copy-start.7 = (f32[2,256,128]{2,1,0:T(8,128)}, f32[2,256,128]{2,1,0:T(8,128)S(1)}, u32[]{:S(2)}) copy-start(f32[2,256,128]{2,1,0:T(8,128)S(1)} %slice_add_fusion.own) | copy-start | bytes 786436
  189.1 19.9 %collective-permute-start.15 = (f32[2,256,128]{2,1,0:T(8,128)S(1)}, f32[2,256,128]{2,1,0:T(8,128)S(1)}, u32[]{:S(2)}, u32[]{:S(2)}) collective-permute-start(f32[2,256,128]{2,1,0:T(8,128)S(1)} %slice_add_fusion.own), channel_id=1, source_target_pairs={{0,1},{1,0},{2,3},{3,2},{4,5},{5,4},{6,7},{7,6},{8,9},{9,8},{10,11... | collective-permute-start | bytes 786440 | tf_op jit(solution)/shard_map/ppermute | solution.py:394
  189.5 18.8 %copy-start.13 = (f32[2,256,128]{2,1,0:T(8,128)S(1)}, f32[2,256,128]{2,1,0:T(8,128)}, u32[]{:S(2)}) copy-start(f32[2,256,128]{2,1,0:T(8,128)} %get-tuple-element.53) | copy-start | bytes 786436
  208.4 9.0 %collective-permute-start.16 = (f32[2,256,128]{2,1,0:T(8,128)S(1)}, f32[2,256,128]{2,1,0:T(8,128)S(1)}, u32[]{:S(2)}, u32[]{:S(2)}) collective-permute-start(f32[2,256,128]{2,1,0:T(8,128)S(1)} %copy-done.13), channel_id=1, source_target_pairs={{2,0},{10,8},{18,16},{26,24},{3,1},{11,9},{19,17},{27,25}} | collective-permute-start | bytes 786440 | tf_op jit(solution)/shard_map/ppermute | solution.py:391
  216.0 107.7 %collective-permute-start.17 = (f32[2,256,128]{2,1,0:T(8,128)}, f32[2,256,128]{2,1,0:T(8,128)S(1)}, u32[]{:S(2)}, u32[]{:S(2)}) collective-permute-start(f32[2,256,128]{2,1,0:T(8,128)} %get-tuple-element.54), channel_id=1, source_target_pairs={{6,4},{14,12},{22,20},{30,28},{7,5},{15,13},{23,21},{31,29}} | collective-permute-start | bytes 786440 | tf_op jit(solution)/shard_map/ppermute | solution.py:391
  (8 other events, 12.8 us)
